TPU v7x, 128 devices: a whole 4x4x4 slice. The times are simulated.
128 devices in a mesh: tm: 8 (over x, core), col: 16 (over z, y).
Axes of the slice: x: 4, y: 4, z: 4, core: 2. Of those that a mesh axis runs over, the one named last changes fastest.
Arguments:
- interior: float32 [8, 2048, 2048], P('tm', None, 'col'), may hold values from -1 to 10, as said below
- left_coupling: float32 [8, 2048, 2048], P('tm', None, 'col'), may hold values from -0.25 to 0.25
- right_coupling: float32 [8, 2048, 2048], P('tm', None, 'col'), may hold values from -0.25 to 0.25
- effects_rows: float32 [8, 64, 2048], P('tm'), may hold values from -0.25 to 0.25
- separator: float32 [8, 2048, 2048], P('tm', None, 'col'), may hold values from -6 to 6
- separator_effects: float32 [8, 64, 2048], P('tm', None, 'col'), may hold values from -1.5 to 1.5
- effects_tip: float32 [64, 64], replicated, may hold values from -6 to 6
Outputs:
- factor: float32 [8, 2048, 2048], P('tm', None, 'col')
- separator_diagonal: float32 [8, 2048, 2048], P('tm', None, 'col')
- separator_coupling: float32 [8, 2048, 2048], P('tm', None, 'col')
- separator_arrow: float32 [8, 64, 2048], P('tm', None, 'col')
- updated_tip: float32 [64, 64], replicated
Inputs may be any that keep to these rules, and one draw needn't show every extreme that they name: Each interior block is symmetric with diagonal entries of 3 or more and a small off-diagonal part, so it is positive definite.
All inputs are finite; a program needn't handle non-finite values.
Results may differ from a plain program's by a relative error of at most 0.000073.
Values sent between devices are 32-bit elements; how exact they have to be, the bound alone decides.
A program may use at most 192 MiB of HBM per device.

v0:
```python
import jax
import jax.numpy as jnp
from jax import lax
from jax.sharding import PartitionSpec as P


def broadcast(value, axis, source):
    kept = jnp.where(lax.axis_index(axis) == source, value, 0).astype(value.dtype)
    return lax.psum(kept, axis)


def shifted(array, axis, by):
    count = lax.axis_size(axis)
    pairs = [(i, i + by) for i in range(count) if 0 <= i + by < count]
    return lax.ppermute(array, axis, pairs)


def product(left, right):
    return jnp.dot(left, right, precision=lax.Precision.HIGHEST, preferred_element_type=jnp.float32)


def local(
    interior, left_coupling, right_coupling, effects_rows, separator, separator_effects, effects_tip
):
    remaining = interior[0]
    block_rows, own_width = remaining.shape
    col_count = lax.axis_size("col")
    own_index = lax.axis_index("col")
    solving = jnp.concatenate([left_coupling[0], right_coupling[0], effects_rows[0].T], axis=1)
    factor = jnp.zeros_like(remaining)
    for step in range(col_count):
        begin = step * own_width
        column = broadcast(remaining[begin:], "col", step)
        corner = jnp.linalg.cholesky(column[:own_width])
        lower_part = lax.linalg.triangular_solve(
            corner, column[own_width:], left_side=False, lower=True, transpose_a=True
        )
        placed = factor.at[begin:].set(jnp.concatenate([corner, lower_part], axis=0))
        factor = jnp.where(own_index == step, placed, factor)
        solved_rows = lax.linalg.triangular_solve(
            corner, solving[begin : begin + own_width], left_side=True, lower=True
        )
        solving = solving.at[begin : begin + own_width].set(solved_rows)
        if step + 1 < col_count:
            limit = block_rows - begin - 2 * own_width
            row_offset = jnp.clip(own_index * own_width - begin - own_width, 0, limit)
            own_rows = lax.dynamic_slice_in_dim(lower_part, row_offset, own_width, 0)
            updated = remaining.at[begin + own_width :].add(-product(lower_part, own_rows.T))
            remaining = jnp.where(own_index > step, updated, remaining)
            solving = solving.at[begin + own_width :].add(-product(lower_part, solved_rows))
    left_solved = solving[:, :own_width]
    right_solved = solving[:, own_width : 2 * own_width]
    effects_solved = solving[:, 2 * own_width :]
    effects_gram = product(effects_solved.T, effects_solved)
    updated_tip = effects_tip - lax.psum(effects_gram, "tm")
    right_cross = product(effects_solved.T, right_solved)
    both_solved = jnp.concatenate([left_solved, right_solved], axis=1)
    left_both = product(lax.all_gather(left_solved, "col", axis=1, tiled=True).T, both_solved)
    right_gram = product(lax.all_gather(right_solved, "col", axis=1, tiled=True).T, right_solved)
    left_gram = left_both[:, :own_width]
    cross_gram = left_both[:, own_width:]
    left_cross = product(effects_solved.T, left_solved)
    next_gram, next_cross = shifted((left_gram, left_cross), "tm", -1)
    diagonal_terms = right_gram + next_gram
    separator_diagonal = separator[0] - diagonal_terms
    separator_coupling = -cross_gram
    separator_arrow = separator_effects[0] - right_cross - next_cross
    return (
        factor[None],
        separator_diagonal[None],
        separator_coupling[None],
        separator_arrow[None],
        updated_tip,
    )


def solution(mesh):
    return jax.shard_map(
        local,
        mesh=mesh,
        in_specs=(
            P("tm", None, "col"),
            P("tm", None, "col"),
            P("tm", None, "col"),
            P("tm", None, None),
            P("tm", None, "col"),
            P("tm", None, "col"),
            P(),
        ),
        out_specs=(
            P("tm", None, "col"),
            P("tm", None, "col"),
            P("tm", None, "col"),
            P("tm", None, "col"),
            P(),
        ),
        check_vma=False,
    )
```

profile of v0, /device:TPU:97, one launch (start us, length us, event | category | flops | bytes accessed | tf_op | source)
XLA Modules:
  0.0 2075.4 jit_solution(13128026291460039475)
XLA Ops:
  14.6 82.9 %all-reduce.17.cloned.1.call-done = f32[2048,128]{0,1:T(8,128)} async-done(((f32[2048,128]{0,1:T(8,128)}), f32[2048,128]{0,1:T(8,128)}) %all-reduce.17.cloned.1.call-update) | async-done | bytes 1048592 | tf_op jit(solution)/shard_map/psum | solution.py:9
  134.7 79.7 %all-reduce.19.cloned.1.call-done = f32[1920,128]{1,0:T(8,128)} async-done(((f32[1920,128]{1,0:T(8,128)}), f32[1920,128]{1,0:T(8,128)}) %all-reduce.19.cloned.1.call-update) | async-done | bytes 983056 | tf_op jit(solution)/shard_map/psum | solution.py:9
  216.3 11.7 cholesky.265
  253.5 77.6 %all-reduce.21.cloned.1.call-done = f32[1792,128]{1,0:T(8,128)} async-done(((f32[1792,128]{1,0:T(8,128)}), f32[1792,128]{1,0:T(8,128)}) %all-reduce.21.cloned.1.call-update) | async-done | bytes 917520 | tf_op jit(solution)/shard_map/psum | solution.py:9
  333.0 11.7 cholesky.276
  368.0 78.8 %all-reduce.23.cloned.1.call-done = f32[1664,128]{1,0:T(8,128)} async-done(((f32[1664,128]{1,0:T(8,128)}), f32[1664,128]{1,0:T(8,128)}) %all-reduce.23.cloned.1.call-update) | async-done | bytes 851984 | tf_op jit(solution)/shard_map/psum | solution.py:9
  482.7 79.3 %all-reduce.25.cloned.1.call-done = f32[1536,128]{1,0:T(8,128)} async-done(((f32[1536,128]{1,0:T(8,128)}), f32[1536,128]{1,0:T(8,128)}) %all-reduce.25.cloned.1.call-update) | async-done | bytes 786448 | tf_op jit(solution)/shard_map/psum | solution.py:9
  564.0 11.7 cholesky.298
  597.7 78.7 %all-reduce.27.cloned.1.call-done = f32[1408,128]{1,0:T(8,128)} async-done(((f32[1408,128]{1,0:T(8,128)}), f32[1408,128]{1,0:T(8,128)}) %all-reduce.27.cloned.1.call-update) | async-done | bytes 720912 | tf_op jit(solution)/shard_map/psum | solution.py:9
  711.4 79.1 %all-reduce.29.cloned.1.call-done = f32[1280,128]{1,0:T(8,128)} async-done(((f32[1280,128]{1,0:T(8,128)}), f32[1280,128]{1,0:T(8,128)}) %all-reduce.29.cloned.1.call-update) | async-done | bytes 655376 | tf_op jit(solution)/shard_map/psum | solution.py:9
  824.6 79.7 %all-reduce.31.cloned.1.call-done = f32[1152,128]{1,0:T(8,128)} async-done(((f32[1152,128]{1,0:T(8,128)}), f32[1152,128]{1,0:T(8,128)}) %all-reduce.31.cloned.1.call-update) | async-done | bytes 589840 | tf_op jit(solution)/shard_map/psum | solution.py:9
  938.0 80.1 %all-reduce.33.cloned.1.call-done = f32[1024,128]{1,0:T(8,128)} async-done(((f32[1024,128]{1,0:T(8,128)}), f32[1024,128]{1,0:T(8,128)}) %all-reduce.33.cloned.1.call-update) | async-done | bytes 524304 | tf_op jit(solution)/shard_map/psum | solution.py:9
  1052.2 79.2 %all-reduce.35.cloned.1.call-done = f32[896,128]{1,0:T(8,128)} async-done(((f32[896,128]{1,0:T(8,128)}), f32[896,128]{1,0:T(8,128)}) %all-reduce.35.cloned.1.call-update) | async-done | bytes 458768 | tf_op jit(solution)/shard_map/psum | solution.py:9
  1163.9 79.6 %all-reduce.37.cloned.1.call-done = f32[768,128]{1,0:T(8,128)} async-done(((f32[768,128]{1,0:T(8,128)}), f32[768,128]{1,0:T(8,128)}) %all-reduce.37.cloned.1.call-update) | async-done | bytes 393232 | tf_op jit(solution)/shard_map/psum | solution.py:9
  1275.9 79.1 %all-reduce.39.cloned.1.call-done = f32[640,128]{1,0:T(8,128)} async-done(((f32[640,128]{1,0:T(8,128)}), f32[640,128]{1,0:T(8,128)}) %all-reduce.39.cloned.1.call-update) | async-done | bytes 327696 | tf_op jit(solution)/shard_map/psum | solution.py:9
  1387.9 79.8 %all-reduce.41.cloned.1.call-done = f32[512,128]{1,0:T(8,128)} async-done(((f32[512,128]{1,0:T(8,128)}), f32[512,128]{1,0:T(8,128)}) %all-reduce.41.cloned.1.call-update) | async-done | bytes 262160 | tf_op jit(solution)/shard_map/psum | solution.py:9
  1498.6 80.8 %all-reduce.43.cloned.1.call-done = f32[384,128]{1,0:T(8,128)} async-done(((f32[384,128]{1,0:T(8,128)}), f32[384,128]{1,0:T(8,128)}) %all-reduce.43.cloned.1.call-update) | async-done | bytes 196624 | tf_op jit(solution)/shard_map/psum | solution.py:9
  1608.9 79.9 %all-reduce.45.cloned.1.call-done = f32[256,128]{1,0:T(8,128)} async-done(((f32[256,128]{1,0:T(8,128)}), f32[256,128]{1,0:T(8,128)}) %all-reduce.45.cloned.1.call-update) | async-done | bytes 131088 | tf_op jit(solution)/shard_map/psum | solution.py:9
  1718.0 79.6 %all-reduce.47.cloned.1.call-done = f32[128,128]{1,0:T(8,128)} async-done(((f32[128,128]{1,0:T(8,128)}), f32[128,128]{1,0:T(8,128)}) %all-reduce.47.cloned.1.call-update) | async-done | bytes 65552 | tf_op jit(solution)/shard_map/psum | solution.py:9
  1869.9 67.9 %all-gather.5.cloned.1.call-done = f32[2048,2048]{0,1:T(8,128)} async-done(((f32[2048,128]{0,1:T(8,128)}), f32[2048,2048]{0,1:T(8,128)}) %all-gather.5.cloned.1.call-update) | async-done | bytes 16777232 | tf_op jit(solution)/shard_map/all_gather | solution.py:58
  1937.8 16.6 fusion.23
  1967.8 23.9 %psum.135 = f32[64,64]{1,0:T(8,128)S(1)} all-reduce(f32[64,64]{1,0:T(8,128)S(1)} %fusion.71), channel_id=1, replica_groups=mesh['tm'=8,'col'=16] {'tm'}, use_global_device_ids=true, to_apply=%region_18.21 | all-reduce | flops 4096 | bytes 32768 | tf_op jit(solution)/shard_map/psum | solution.py:55
  1994.1 57.0 %all-gather.3.cloned.1.call-done = f32[2048,2048]{0,1:T(8,128)} async-done(((f32[2048,128]{0,1:T(8,128)}), f32[2048,2048]{0,1:T(8,128)}) %all-gather.3.cloned.1.call-update) | async-done | bytes 16777232 | tf_op jit(solution)/shard_map/all_gather | solution.py:59
  2051.1 16.9 fusion.22
  (411 shorter events, 567.7 us)
Async XLA Ops:
  7.2 90.3 %all-reduce.17.cloned.1.call-start = ((), (), s32[]{:S(2)}) async-start(), calls=%async_computation | async-start | bytes 2097152 | tf_op jit(solution)/shard_map/psum | solution.py:9
  10.0 204.4 %all-reduce.19.cloned.1.call-start = ((), (), s32[]{:S(2)}) async-start(), calls=%async_computation.1 | async-start | bytes 1966080 | tf_op jit(solution)/shard_map/psum | solution.py:9
  129.0 202.1 %all-reduce.21.cloned.1.call-start = ((), (), s32[]{:S(2)}) async-start(), calls=%async_computation.2 | async-start | bytes 1835008 | tf_op jit(solution)/shard_map/psum | solution.py:9
  245.8 201.0 %all-reduce.23.cloned.1.call-start = ((), (), s32[]{:S(2)}) async-start(), calls=%async_computation.3 | async-start | bytes 1703936 | tf_op jit(solution)/shard_map/psum | solution.py:9
  361.7 200.4 %all-reduce.25.cloned.1.call-start = ((), (), s32[]{:S(2)}) async-start(), calls=%async_computation.4 | async-start | bytes 1572864 | tf_op jit(solution)/shard_map/psum | solution.py:9
  476.6 199.9 %all-reduce.27.cloned.1.call-start = ((), (), s32[]{:S(2)}) async-start(), calls=%async_computation.5 | async-start | bytes 1441792 | tf_op jit(solution)/shard_map/psum | solution.py:9
  591.7 198.8 %all-reduce.29.cloned.1.call-start = ((), (), s32[]{:S(2)}) async-start(), calls=%async_computation.6 | async-start | bytes 1310720 | tf_op jit(solution)/shard_map/psum | solution.py:9
  705.8 198.5 %all-reduce.31.cloned.1.call-start = ((), (), s32[]{:S(2)}) async-start(), calls=%async_computation.7 | async-start | bytes 1179648 | tf_op jit(solution)/shard_map/psum | solution.py:9
  819.7 198.4 %all-reduce.33.cloned.1.call-start = ((), (), s32[]{:S(2)}) async-start(), calls=%async_computation.8 | async-start | bytes 1048576 | tf_op jit(solution)/shard_map/psum | solution.py:9
  933.3 198.1 %all-reduce.35.cloned.1.call-start = ((), (), s32[]{:S(2)}) async-start(), calls=%async_computation.9 | async-start | bytes 917504 | tf_op jit(solution)/shard_map/psum | solution.py:9
  1047.4 196.1 %all-reduce.37.cloned.1.call-start = ((), (), s32[]{:S(2)}) async-start(), calls=%async_computation.10 | async-start | bytes 786432 | tf_op jit(solution)/shard_map/psum | solution.py:9
  1159.7 195.3 %all-reduce.39.cloned.1.call-start = ((), (), s32[]{:S(2)}) async-start(), calls=%async_computation.11 | async-start | bytes 655360 | tf_op jit(solution)/shard_map/psum | solution.py:9
  1271.9 195.8 %all-reduce.41.cloned.1.call-start = ((), (), s32[]{:S(2)}) async-start(), calls=%async_computation.12 | async-start | bytes 524288 | tf_op jit(solution)/shard_map/psum | solution.py:9
  1383.9 195.5 %all-reduce.43.cloned.1.call-start = ((), (), s32[]{:S(2)}) async-start(), calls=%async_computation.13 | async-start | bytes 393216 | tf_op jit(solution)/shard_map/psum | solution.py:9
  1496.4 192.5 %all-reduce.45.cloned.1.call-start = ((), (), s32[]{:S(2)}) async-start(), calls=%async_computation.14 | async-start | bytes 262144 | tf_op jit(solution)/shard_map/psum | solution.py:9
  1497.2 108.7 %copy-start.36 = (f32[384,128]{1,0:T(8,128)S(1)}, f32[384,128]{1,0:T(8,128)}, u32[]{:S(2)}) copy-start(f32[384,128]{1,0:T(8,128)} %get-tuple-element.825) | copy-start | bytes 589828
  1606.9 109.2 %copy-start.38 = (f32[256,128]{1,0:T(8,128)S(1)}, f32[256,128]{1,0:T(8,128)}, u32[]{:S(2)}) copy-start(f32[256,128]{1,0:T(8,128)} %get-tuple-element.827) | copy-start | bytes 393220
  1607.0 190.6 %all-reduce.47.cloned.1.call-start = ((), (), s32[]{:S(2)}) async-start(), calls=%async_computation.15 | async-start | bytes 131072 | tf_op jit(solution)/shard_map/psum | solution.py:9
  1608.9 215.9 %copy-start.29 = (f32[384,128]{1,0:T(8,128)}, f32[384,128]{1,0:T(8,128)S(1)}, u32[]{:S(2)}) copy-start(f32[384,128]{1,0:T(8,128)S(1)} %slice_select_fusion.11) | copy-start | bytes 589828
  1717.0 220.8 %all-gather.5.cloned.1.call-start = ((), (), s32[]{:S(2)}) async-start(), calls=%async_computation.17 | async-start | bytes 17825792 | tf_op jit(solution)/shard_map/all_gather | solution.py:58
  1717.6 107.2 %copy-start.33 = (f32[256,128]{1,0:T(8,128)}, f32[256,128]{1,0:T(8,128)S(1)}, u32[]{:S(2)}) copy-start(f32[256,128]{1,0:T(8,128)S(1)} %slice_select_fusion.12) | copy-start | bytes 393220
  1824.8 226.3 %all-gather.3.cloned.1.call-start = ((), (), s32[]{:S(2)}) async-start(), calls=%async_computation.16 | async-start | bytes 17825792 | tf_op jit(solution)/shard_map/all_gather | solution.py:59
  1955.9 95.2 %collective-permute-start = (f32[2048,128]{1,0:T(8,128)}, f32[2048,128]{1,0:T(8,128)}, u32[]{:S(2)}, u32[]{:S(2)}) collective-permute-start(f32[2048,128]{1,0:T(8,128)} %get-tuple-element.797), channel_id=1, source_target_pairs={{16,0},{32,16},{48,32},{64,48},{80,64},{96,80},{112,96},{17,1},{33... | collective-permute-start | bytes 3145736 | tf_op jit(solution)/shard_map/ppermute | solution.py:15
  1962.1 30.2 %collective-permute-start.1 = (f32[64,128]{1,0:T(8,128)S(1)}, f32[64,128]{1,0:T(8,128)S(1)}, u32[]{:S(2)}, u32[]{:S(2)}) collective-permute-start(f32[64,128]{1,0:T(8,128)S(1)} %fusion.73), channel_id=1, source_target_pairs={{16,0},{32,16},{48,32},{64,48},{80,64},{96,80},{112,96},{17,1},{33... | collective-permute-start | bytes 98312 | tf_op jit(solution)/shard_map/ppermute | solution.py:15
  (44 other events, 186.7 us)
Sparse Core Ops, SparseCore 0:
  11.8 85.6 all-reduce.16
  129.1 85.2 all-reduce.18
  245.9 85.1 all-reduce.20
  361.8 84.9 all-reduce.22
  476.7 85.3 all-reduce.24
  591.8 84.6 all-reduce.26
  706.0 84.5 all-reduce.28
  819.8 84.4 all-reduce.30
  933.4 84.6 all-reduce.32
  1047.5 83.8 all-reduce.34
  1159.8 83.6 all-reduce.36
  1272.0 82.9 all-reduce.38
  1384.0 83.6 all-reduce.40
  1496.5 82.8 all-reduce.42
  1607.1 81.6 all-reduce.44
  1717.2 80.3 all-reduce.46
  1824.9 112.8 all-gather.4
  1940.0 111.0 all-gather.2
where the time goes:
time: 2090 us; the launch traced here: 2080 us
  waiting for transfers between devices  1400 us (67%)
  other arithmetic  408 us (20%)
  matrix products  132 us (6%)
  local copies, waits for them, and re-layouts  86.5 us (4%)
  blocking collectives  23.9 us (1%)
    psum x16, waiting for transfers between devices, broadcast(): return lax.psum(kept, axis)  1270 us
    another operation x48, other arithmetic, local(): corner = jnp.linalg.cholesky(column[:own_width])  198 us
    another operation x30, other arithmetic, local(): lax.linalg.triangular_solve(corner, column[own_width:], left_side=False,...  164 us
    dot_general x35, matrix products, product(): jnp.dot(left, right, precision=lax.Precision.HIGHEST, preferred_element_t...  91.8 us
    all_gather x1, waiting for transfers between devices, local(): lax.all_gather(left_solved, 'col', axis=1, tiled=True)  67.9 us
    all_gather x1, waiting for transfers between devices, local(): lax.all_gather(right_solved, 'col', axis=1, tiled=True)  57 us
  transfers between devices with their start and end apart: 20, of which 18 were waited for; matrix products, arithmetic and copies ran while one was open for 6% of the time, Pallas kernels for 0%

commit v1 on v0

v1 whole, which is shorter than its diff:
```python
import jax
import jax.numpy as jnp
from jax import lax
from jax.experimental import pallas as pl
from jax.experimental.pallas import tpu as pltpu
from jax.sharding import PartitionSpec as P

W = 128
N = 16
B = N * W
NF = 64
X0 = B
XW = 3 * W
TILES = N * (N + 1) // 2
MESH = pl.DeviceIdType.MESH
F32, BF16 = jnp.float32, jnp.bfloat16
OFFSETS = ((0, 1), (1, 0), (3, 3), (3, 1), (1, 2), (2, 3), (0, 2), (2, 0), (2, 2))
FULL = 6


def split(x):
    high = x.astype(BF16)
    return high, (x - high.astype(F32)).astype(BF16)


def dot3(a_high, a_low, b_high, b_low):
    def one(a, b):
        return jnp.dot(a, b, preferred_element_type=F32)

    return one(a_high, b_high) + (one(a_high, b_low) + one(a_low, b_high))


def corner(rows):
    lane = lax.broadcasted_iota(jnp.int32, (8, W), 1)
    sub = lax.broadcasted_iota(jnp.int32, (8, W), 0)
    first = lane[0:1]
    rows = list(rows)
    upper, inverse = [], []

    def lanes(x, c):
        return jnp.broadcast_to(x[:, c : c + 1], (8, W))

    for s in range(W // 8):
        r = 8 * s
        block = rows[s]
        c = [lanes(block, r + j) for j in range(8)]
        e = {(i, j): c[j][i : i + 1, :] for j in range(8) for i in range(j, 8)}
        inv, low = [None] * 8, {}
        for j in range(8):
            inv[j] = lax.rsqrt(e[j, j])
            for i in range(j + 1, 8):
                low[i, j] = e[i, j] * inv[j]
            for i in range(j + 1, 8):
                for m in range(j + 1, i + 1):
                    e[i, m] = e[i, m] - low[i, j] * low[m, j]
        diagonal = (lane >= r) & (lane < r + 8)
        own = jnp.where(diagonal, (lane - r == sub).astype(F32), block)
        u = []
        for j in range(8):
            t = own[j : j + 1, :]
            for m in range(j):
                t = t - low[j, m] * u[m]
            u.append(t * inv[j])
        z = [None] * 8
        for j in reversed(range(8)):
            t = u[j]
            for m in range(j + 1, 8):
                t = t - low[m, j] * z[m]
            z[j] = t * inv[j]
        solved = jnp.concatenate(u, axis=0)
        small = jnp.zeros((8, W), F32)
        for j in range(8):
            t = jnp.where(first == r + j, e[j, j] * inv[j], 0.0)
            for m in range(j + 1, 8):
                t = jnp.where(first == r + m, low[m, j], t)
            small = jnp.where(sub == j, t, small)
        upper.append(jnp.where(lane >= r + 8, solved, small))
        inverse.append(jnp.where(lane < r + 8, solved, 0.0))
        z = [jnp.broadcast_to(t, (8, W)) for t in z]
        for i in range(s + 1, W // 8):
            t = jnp.where(diagonal, 0.0, rows[i])
            for j in range(8):
                t = t - lanes(rows[i], r + j) * z[j]
            rows[i] = t
    return upper, inverse


def tile(k, j):
    return k * (2 * N + 1 - k) // 2 + j - k


def at(i, size=W):
    return pl.ds(pl.multiple_of(i * size, size), size)


def kernel(
    a, left, right, effects, separator, separator_effects, tip,
    factor, diagonal_out, coupling_out, arrow_out, tip_out,
    tiles, high, low, panel, corner_up, corner_inv, x_own, x_got, xt_high, xt_low, self_gram,
    result_got, next_got, cross_got, tip_got, tip_own, cross_own,
    tile_send, tile_recv, x_send, x_recv, result_send, result_recv,
    next_send, next_recv, cross_send, cross_recv, tip_send, tip_recv,
):
    me = lax.axis_index("col")
    tm = lax.axis_index("tm")
    tms = lax.axis_size("tm")
    z, y = me // 4, me % 4

    def moved(dz, dy):
        return ((z + dz + 4) % 4) * 4 + (y + dy + 4) % 4

    barrier = pltpu.get_barrier_semaphore()

    def greet(o, _):
        pl.semaphore_signal(barrier, inc=1, device_id={"tm": tm, "col": (me + o) % N}, device_id_type=MESH)
        return 0

    lax.fori_loop(1, N, greet, 0)

    def greet_tm(o, _):
        pl.semaphore_signal(barrier, inc=1, device_id={"tm": (tm + o) % tms, "col": me}, device_id_type=MESH)
        return 0

    lax.fori_loop(1, tms, greet_tm, 0)
    pl.semaphore_wait(barrier, N - 1 + tms - 1)

    def tile_copy(k, o):
        to = ((z + o // 4) % 4) * 4 + (y + o % 4) % 4
        return pltpu.make_async_remote_copy(
            src_ref=a.at[at(k)], dst_ref=tiles.at[tile(k, me)],
            send_sem=tile_send.at[k, o], recv_sem=tile_recv.at[tile(k, me)],
            device_id={"tm": tm, "col": to}, device_id_type=MESH,
        )

    def tile_arrival(k, j):
        return pltpu.make_async_remote_copy(
            src_ref=a.at[at(k)], dst_ref=tiles.at[tile(k, j)],
            send_sem=tile_send.at[k, 1], recv_sem=tile_recv.at[tile(k, j)],
            device_id={"tm": tm, "col": (me + 1) % N}, device_id_type=MESH,
        )

    def send_tiles(k, _):
        def to_one(o, _):
            tile_copy(k, o).start()
            return 0

        lax.fori_loop(1, N, to_one, 0)
        tiles[tile(k, me)] = a[at(k), :]
        return 0

    lax.fori_loop(0, me + 1, send_tiles, 0)

    def clear(k, _):
        high[at(k), :] = jnp.zeros((W, B + XW), BF16)
        low[at(k), :] = jnp.zeros((W, B + XW), BF16)
        factor[at(k), :] = jnp.zeros((W, W), F32)
        return 0

    lax.fori_loop(0, N, clear, 0)

    own_bit = (y // 2, z // 2, z // 2)

    def slot(d, k):
        return d * N + k if d < FULL else FULL * N + (d - FULL) * (N // 2) + k // 2

    def x_copy(d, k):
        return pltpu.make_async_remote_copy(
            src_ref=x_own.at[at(k)], dst_ref=x_got.at[slot(d, k)],
            send_sem=x_send.at[slot(d, k)], recv_sem=x_recv.at[slot(d, k)],
            device_id={"tm": tm, "col": moved(*OFFSETS[d])}, device_id_type=MESH,
        )

    def updated(k, begin, width):
        def add(kk, total):
            return total + dot3(
                high[at(k), at(kk, 2 * W)], low[at(k), at(kk, 2 * W)],
                high[at(kk, 2 * W), pl.ds(begin, width)], low[at(kk, 2 * W), pl.ds(begin, width)],
            )

        return lax.fori_loop(0, (k + 1) // 2, add, jnp.zeros((W, width), F32))

    def step(k, _):
        def wait_tile(j, _):
            @pl.when(j != me)
            def _():
                tile_arrival(k, j).wait_recv()

            return 0

        lax.fori_loop(k, N, wait_tile, 0)

        def update_four(c, _):
            begin = pl.multiple_of(c * 4 * W, 4 * W)
            total = updated(k, begin, 4 * W)
            for i in range(4):
                j = c * 4 + i

                @pl.when(j >= k)
                def _():
                    panel[:, at(j)] = tiles[tile(k, jnp.maximum(j, k))] - total[:, i * W : (i + 1) * W]

            return 0

        lax.fori_loop(k // 4, N // 4, update_four, 0)
        total = updated(k, X0, XW)
        panel[:, X0 : X0 + W] = left[at(k), :] - total[:, :W]
        panel[:, X0 + W : X0 + 2 * W] = right[at(k), :] - total[:, W : 2 * W]
        rows = jnp.concatenate([effects[:, at(k)], jnp.zeros((W - NF, W), F32)], axis=0)
        panel[:, X0 + 2 * W :] = rows.T - total[:, 2 * W :]

        upper, inverse = corner([panel[8 * i : 8 * i + 8, at(k)] for i in range(W // 8)])
        for i in range(W // 8):
            corner_up[8 * i : 8 * i + 8, :] = upper[i]
            corner_inv[8 * i : 8 * i + 8, :] = inverse[i]

        @pl.when(me == k)
        def _():
            factor[at(k), :] = corner_up[...].T

        inv_high, inv_low = split(corner_inv[...])

        def solve_four(c, _):
            begin = pl.multiple_of(c * 4 * W, 4 * W)
            part = dot3(inv_high, inv_low, *split(panel[:, pl.ds(begin, 4 * W)]))
            for i in range(4):
                j = c * 4 + i

                @pl.when(j > k)
                def _():
                    one = part[:, i * W : (i + 1) * W]
                    high[at(k), at(j)], low[at(k), at(j)] = split(one)
                    turned = one.T
                    high[at(j), at(k)], low[at(j), at(k)] = split(turned)

                    @pl.when(me == k)
                    def _():
                        factor[at(j), :] = turned

            return 0

        lax.fori_loop(k // 4, N // 4, solve_four, 0)
        part = dot3(inv_high, inv_low, *split(panel[:, X0:]))
        x_own[at(k), :] = part[:, : 2 * W]
        high[at(k), X0:], low[at(k), X0:] = split(part)
        for i in range(3):
            rows = slice(i * W, (i + 1) * W)
            xt_high[rows, at(k)], xt_low[rows, at(k)] = split(part[:, rows].T)
        for d in range(len(OFFSETS)):
            if d < FULL:
                x_copy(d, k).start()
            else:

                @pl.when((k + own_bit[d - FULL]) % 2 == 0)
                def _():
                    x_copy(d, k).start()

        return 0

    lax.fori_loop(0, N, step, 0)

    self_gram[...] = jnp.zeros((XW, XW), F32)

    def clear_gram(i, _):
        tiles[i] = jnp.zeros((W, W), F32)
        return 0

    lax.fori_loop(0, 4 * len(OFFSETS), clear_gram, 0)

    def add_gram(d, k, got):
        part = dot3(xt_high[: 2 * W, k], xt_low[: 2 * W, k], *split(got))
        tiles[4 * d] += part[:W, :W]
        tiles[4 * d + 1] += part[:W, W:]
        tiles[4 * d + 2] += part[W:, W:]
        tiles[4 * d + 3] += part[W:, :W]

    def gram_step(p, _):
        pair = at(p, 2 * W)
        self_gram[...] += dot3(xt_high[:, pair], xt_low[:, pair], high[pair, X0:], low[pair, X0:])
        for d in range(len(OFFSETS)):
            if d < FULL:
                x_copy(d, 2 * p).wait_recv()
                x_copy(d, 2 * p + 1).wait_recv()
                got = x_got[pl.ds(d * N + 2 * p, 2)].reshape(2 * W, 2 * W)
                add_gram(d, pair, got)
            else:
                k = 2 * p + 1 - own_bit[d - FULL]
                x_copy(d, k).wait_recv()
                add_gram(d, at(k), x_got[slot(d, k)])
        return 0

    lax.fori_loop(0, N // 2, gram_step, 0)

    def result_copy(d):
        dz, dy = OFFSETS[d]
        return pltpu.make_async_remote_copy(
            src_ref=tiles.at[pl.ds(4 * d, 3)], dst_ref=result_got.at[d],
            send_sem=result_send.at[d], recv_sem=result_recv.at[d],
            device_id={"tm": tm, "col": moved(-dz, -dy)}, device_id_type=MESH,
        )

    for d in range(len(OFFSETS)):
        result_copy(d).start()

    cross_own[...] = self_gram[2 * W : 2 * W + NF, :W]
    tip_own[...] = self_gram[2 * W : 2 * W + NF, 2 * W :]

    def tip_copy(o):
        return pltpu.make_async_remote_copy(
            src_ref=tip_own, dst_ref=tip_got.at[o],
            send_sem=tip_send.at[o], recv_sem=tip_recv.at[o],
            device_id={"tm": (tm + o) % tms, "col": me}, device_id_type=MESH,
        )

    for o in range(1, tms):
        tip_copy(o).start()

    back = {"tm": (tm + tms - 1) % tms, "col": me}
    cross_copy = pltpu.make_async_remote_copy(
        src_ref=cross_own, dst_ref=cross_got, send_sem=cross_send, recv_sem=cross_recv,
        device_id=back, device_id_type=MESH,
    )

    @pl.when(tm > 0)
    def _():
        cross_copy.start()

    base = 4 * len(OFFSETS)

    def next_copy(b):
        return pltpu.make_async_remote_copy(
            src_ref=tiles.at[base + b], dst_ref=next_got.at[b],
            send_sem=next_send.at[b], recv_sem=next_recv.at[b],
            device_id=back, device_id_type=MESH,
        )

    def block_out(b, left_gram, cross_gram, right_gram):
        tiles[base + b] = left_gram

        @pl.when(tm > 0)
        def _():
            next_copy(b).start()

        coupling_out[at(b), :] = -cross_gram
        diagonal_out[at(b), :] = separator[at(b), :] - right_gram

    block_out(me, self_gram[:W, :W], self_gram[:W, W : 2 * W], self_gram[W : 2 * W, W : 2 * W])
    for d in range(FULL):
        dz, dy = OFFSETS[d]
        block_out(moved(-dz, -dy), tiles[4 * d].T, tiles[4 * d + 3].T, tiles[4 * d + 2].T)
    for d in range(len(OFFSETS)):
        result_copy(d).wait_recv()
        got = [result_got[d, i] for i in range(3)]
        if d >= FULL:
            got = [got[0] + tiles[4 * d].T, got[1] + tiles[4 * d + 3].T, got[2] + tiles[4 * d + 2].T]
        block_out(moved(*OFFSETS[d]), *got)

    total = self_gram[2 * W : 2 * W + NF, 2 * W :]
    for o in range(1, tms):
        tip_copy(o).wait_recv()
        total = total + tip_got[o]
    tip_out[...] = tip[...] - total[:, :NF]

    arrow_out[...] = separator_effects[...] - self_gram[2 * W : 2 * W + NF, W : 2 * W]

    @pl.when(tm < tms - 1)
    def _():
        cross_copy.wait_recv()
        arrow_out[...] -= cross_got[...]

        def add_next(b, _):
            next_copy(b).wait_recv()
            diagonal_out[at(b), :] -= next_got[b]
            return 0

        lax.fori_loop(0, N, add_next, 0)

    def drain_tiles(k, _):
        def one(o, _):
            tile_copy(k, o).wait_send()
            return 0

        lax.fori_loop(1, N, one, 0)
        return 0

    lax.fori_loop(0, me + 1, drain_tiles, 0)
    for d in range(len(OFFSETS)):
        if d < FULL:

            def drain_x(k, _):
                x_copy(d, k).wait_send()
                return 0

            lax.fori_loop(0, N, drain_x, 0)
        else:

            def drain_half(p, _):
                x_copy(d, 2 * p + own_bit[d - FULL]).wait_send()
                return 0

            lax.fori_loop(0, N // 2, drain_half, 0)
        result_copy(d).wait_send()
    for o in range(1, tms):
        tip_copy(o).wait_send()

    @pl.when(tm > 0)
    def _():
        cross_copy.wait_send()

        def drain_next(b, _):
            next_copy(b).wait_send()
            return 0

        lax.fori_loop(0, N, drain_next, 0)


def local(interior, left, right, effects, separator, separator_effects, tip):
    tms = lax.axis_size("tm")
    dma = pltpu.SemaphoreType.DMA
    copies = FULL * N + 3 * (N // 2)
    vmem = pl.BlockSpec(memory_space=pltpu.VMEM)
    outputs = pl.pallas_call(
        kernel,
        out_shape=(
            jax.ShapeDtypeStruct((B, W), F32),
            jax.ShapeDtypeStruct((B, W), F32),
            jax.ShapeDtypeStruct((B, W), F32),
            jax.ShapeDtypeStruct((NF, W), F32),
            jax.ShapeDtypeStruct((NF, NF), F32),
        ),
        in_specs=[vmem] * 7,
        out_specs=[vmem] * 5,
        scratch_shapes=[
            pltpu.VMEM((TILES, W, W), F32),
            pltpu.VMEM((B, B + XW), BF16),
            pltpu.VMEM((B, B + XW), BF16),
            pltpu.VMEM((W, B + XW), F32),
            pltpu.VMEM((W, W), F32),
            pltpu.VMEM((W, W), F32),
            pltpu.VMEM((B, 2 * W), F32),
            pltpu.VMEM((copies, W, 2 * W), F32),
            pltpu.VMEM((XW, B), BF16),
            pltpu.VMEM((XW, B), BF16),
            pltpu.VMEM((XW, XW), F32),
            pltpu.VMEM((len(OFFSETS), 3, W, W), F32),
            pltpu.VMEM((N, W, W), F32),
            pltpu.VMEM((NF, W), F32),
            pltpu.VMEM((8, NF, W), F32),
            pltpu.VMEM((NF, W), F32),
            pltpu.VMEM((NF, W), F32),
            dma((N, N)),
            dma((TILES,)),
            dma((copies,)),
            dma((copies,)),
            dma((len(OFFSETS),)),
            dma((len(OFFSETS),)),
            dma((N,)),
            dma((N,)),
            dma(()),
            dma(()),
            dma((8,)),
            dma((8,)),
        ],
        compiler_params=pltpu.CompilerParams(
            collective_id=0, has_side_effects=True, vmem_limit_bytes=64 * 1024 * 1024 - 65536
        ),
        name="eliminate",
    )(interior[0], left[0], right[0], effects[0], separator[0], separator_effects[0], tip)
    return tuple(x[None] for x in outputs[:4]) + (outputs[4],)


def solution(mesh):
    return jax.shard_map(
        local,
        mesh=mesh,
        in_specs=(
            P("tm", None, "col"),
            P("tm", None, "col"),
            P("tm", None, "col"),
            P("tm", None, None),
            P("tm", None, "col"),
            P("tm", None, "col"),
            P(),
        ),
        out_specs=(
            P("tm", None, "col"),
            P("tm", None, "col"),
            P("tm", None, "col"),
            P("tm", None, "col"),
            P(),
        ),
        check_vma=False,
    )
```

time: 2090 us -> 450 us (0.22)
  waiting for transfers between devices: 1400 us -> 0 us
  Pallas kernels: 0 us -> 437 us
  other arithmetic: 408 us -> 0 us
  matrix products: 132 us -> 0 us
  local copies, waits for them, and re-layouts: 86.5 us -> 6.31 us
  blocking collectives: 23.9 us -> 0 us
    psum x16 -> x0, waiting for transfers between devices: 1270 us -> none  [broadcast(): return lax.psum(kept, axis)]
    pallas_call x0 -> x1, Pallas kernels: none -> 437 us  [local(): pl.pallas_call(kernel, out_shape=(jax.ShapeDtypeStruct((B, W), F32), jax....]
    another operation x80 -> x0, other arithmetic: 373 us -> none  [the longest x48 198 us: local(): corner = jnp.linalg.cholesky(column[:own_width])]
    all_gather x2 -> x0, waiting for transfers between devices: 125 us -> none  [the longest x1 67.9 us: local(): lax.all_gather(left_solved, 'col', axis=1, tiled=True)]
    dot_general x35 -> x0, matrix products: 91.8 us -> none  [product(): jnp.dot(left, right, precision=lax.Precision.HIGHEST, preferred_element_t...]
    another operation x31 -> x0, matrix products: 39.7 us -> none  [the longest x15 24.9 us: local(): lax.linalg.triangular_solve(corner, column[own_width:], left_side=False,...]
    psum x1 -> x0, blocking collectives: 23.9 us -> none  [local(): updated_tip = effects_tip - lax.psum(effects_gram, 'tm')]
    select_n x15 -> x0, local copies, waits for them, and re-layouts: 23.8 us -> none  [local(): factor = jnp.where(own_index == step, placed, factor)]
  transfers between devices with their start and end apart: 20 -> 0, of which waited for: 18 -> 0; matrix products, arithmetic and copies ran while one was open for 6% -> 0% of each run, Pallas kernels for 0% -> 0%
where the time goes in v1:
time: 450 us; the launch traced here: 444 us
  Pallas kernels  437 us (97%)
  local copies, waits for them, and re-layouts  6.31 us (1%)
    pallas_call x1, Pallas kernels, local(): pl.pallas_call(kernel, out_shape=(jax.ShapeDtypeStruct((B, W), F32), jax....  437 us

profile of v1, /device:TPU:97, one launch (start us, length us, event | category | flops | bytes accessed | tf_op | source)
XLA Modules:
  0.0 444.1 jit_solution(10525002196990595814)
XLA Ops:
  0.6 437.1 %eliminate.1 = (f32[2048,128]{1,0:T(8,128)}, f32[2048,128]{1,0:T(8,128)}, f32[2048,128]{1,0:T(8,128)}, f32[64,128]{1,0:T(8,128)}, f32[64,64]{1,0:T(8,128)}) custom-call(f32[2048,128]{1,0:T(8,128)} %bitcast.13, f32[2048,128]{1,0:T(8,128)} %bitcast.14, f32[2048,128]{1,0:T(8,128)} %bitcast.15, f32[64,2048]{1,0:T(8,128)} %bitcast.17, f32[2048,128]{1,0:T(8,128)} %bitcast.16, ...), custom_call_target="tpu_custom_call" | custom-call | tf_op jit(solution)/shard_map/eliminate/pallas_call | solution.py:421
  437.8 0.0 copy-start.1
  437.8 2.4 copy.17
  440.1 0.0 copy-done.1
  440.1 0.0 copy-start
  440.1 1.0 copy.18
  441.1 0.6 copy-done
  441.7 0.0 copy-start.3
  441.7 1.0 copy.19
  442.7 0.0 copy-done.3
  442.7 0.0 copy-start.2
  442.7 0.6 copy.20
  443.3 0.2 copy-done.2
  443.5 0.6 copy.21
Async XLA Ops:
  437.8 2.4 copy-start.1
  440.1 1.6 copy-start
  441.7 1.0 copy-start.3
  442.7 0.8 copy-start.2

commit v2 on v1

--- a/solution.py
+++ b/solution.py
@@ -14,8 +14,16 @@
 TILES = N * (N + 1) // 2
 MESH = pl.DeviceIdType.MESH
 F32, BF16 = jnp.float32, jnp.bfloat16
-OFFSETS = ((0, 1), (1, 0), (3, 3), (3, 1), (1, 2), (2, 3), (0, 2), (2, 0), (2, 2))
-FULL = 6
+OFFSETS = ((0, 1), (1, 0), (1, 1), (1, 3), (1, 2), (2, 1), (0, 2), (2, 0), (2, 2))
+BACK = 6
+PEERS = len(OFFSETS)
+TREES = (
+    {0: (-1, 1), 2: (0, 2), 1: (2, 3), 4: (2, 3), 5: (2, 3), 3: (4, 4), 6: (4, 4), 7: (5, 4), 8: (5, 4)},
+    {1: (-1, 1), 2: (1, 2), 3: (1, 2), 0: (2, 3), 4: (3, 3), 5: (2, 3), 6: (4, 4), 7: (5, 4), 8: (4, 4)},
+)
+PASSED = tuple(frozenset(p for p, _ in tree.values()) for tree in TREES)
+DIRECT_X = 14
+DIRECT_A = 5
 
 
 def split(x):
@@ -99,7 +107,7 @@
     tiles, high, low, panel, corner_up, corner_inv, x_own, x_got, xt_high, xt_low, self_gram,
     result_got, next_got, cross_got, tip_got, tip_own, cross_own,
     tile_send, tile_recv, x_send, x_recv, result_send, result_recv,
-    next_send, next_recv, cross_send, cross_recv, tip_send, tip_recv,
+    next_send, next_recv, cross_send, cross_recv, tip_send, tip_recv, separator_sem,
 ):
     me = lax.axis_index("col")
     tm = lax.axis_index("tm")
@@ -124,31 +132,116 @@
     lax.fori_loop(1, tms, greet_tm, 0)
     pl.semaphore_wait(barrier, N - 1 + tms - 1)
 
-    def tile_copy(k, o):
-        to = ((z + o // 4) % 4) * 4 + (y + o % 4) % 4
+    def tile_copy(k, source, index, to):
         return pltpu.make_async_remote_copy(
-            src_ref=a.at[at(k)], dst_ref=tiles.at[tile(k, me)],
-            send_sem=tile_send.at[k, o], recv_sem=tile_recv.at[tile(k, me)],
+            src_ref=tiles.at[tile(k, source)], dst_ref=tiles.at[tile(k, source)],
+            send_sem=tile_send.at[k, index], recv_sem=tile_recv.at[tile(k, source)],
             device_id={"tm": tm, "col": to}, device_id_type=MESH,
         )
 
-    def tile_arrival(k, j):
-        return pltpu.make_async_remote_copy(
-            src_ref=a.at[at(k)], dst_ref=tiles.at[tile(k, j)],
-            send_sem=tile_send.at[k, 1], recv_sem=tile_recv.at[tile(k, j)],
-            device_id={"tm": tm, "col": (me + 1) % N}, device_id_type=MESH,
-        )
-
-    def send_tiles(k, _):
-        def to_one(o, _):
-            tile_copy(k, o).start()
-            return 0
-
-        lax.fori_loop(1, N, to_one, 0)
+    def tile_arrival(k, source):
+        return tile_copy(k, source, 0, (me + 1) % N)
+
+    separator_copy = pltpu.make_async_copy(separator, diagonal_out, separator_sem)
+    separator_copy.start()
+
+    def own_tile(k, _):
         tiles[tile(k, me)] = a[at(k), :]
         return 0
 
-    lax.fori_loop(0, me + 1, send_tiles, 0)
+    lax.fori_loop(0, me + 1, own_tile, 0)
+
+    def direct_tiles(k, action):
+        @pl.when(me >= k)
+        def _():
+            def to_one(o, _):
+                to = ((z + o // 4) % 4) * 4 + (y + o % 4) % 4
+                action(tile_copy(k, me, o - 1, to))
+                return 0
+
+            lax.fori_loop(1, N, to_one, 0)
+
+    def start(copy):
+        copy.start()
+
+    def wait_send(copy):
+        copy.wait_send()
+
+    for k in range(DIRECT_A):
+        direct_tiles(k, start)
+
+    def along(k, first, second):
+        even = 1 - k % 2
+        dz = first * (1 - even) + second * even
+        dy = first * even + second * (1 - even)
+        return ((z + dz + 4) % 4) * 4 + (y + dy + 4) % 4
+
+    def way(k):
+        return 1 - 2 * ((k // 2) % 2)
+
+    def wait_tile(k, source):
+        @pl.when(source >= k)
+        def _():
+            tile_arrival(k, source).wait_recv()
+
+    def forward(k, source, index, to, action):
+        @pl.when(source >= k)
+        def _():
+            action(tile_copy(k, source, index, to))
+
+    def stage_own(k, action, waits):
+        forward(k, me, 0, along(k, 1, 0), action)
+        forward(k, me, 1, along(k, -1, 0), action)
+
+    def stage_next(k, action, waits):
+        source = along(k, -way(k), 0)
+        if waits:
+            wait_tile(k, source)
+        forward(k, source, 2, along(k, way(k), 0), action)
+
+    def stage_line(k, action, waits):
+        if waits:
+            wait_tile(k, along(k, way(k), 0))
+            wait_tile(k, along(k, 2, 0))
+        for i in range(4):
+            source = along(k, i, 0)
+            forward(k, source, 3 + 2 * i, along(k, 0, 1), action)
+            forward(k, source, 4 + 2 * i, along(k, 0, -1), action)
+
+    def stage_last(k, action, waits):
+        for i in range(4):
+            source = along(k, i, -way(k))
+            if waits:
+                wait_tile(k, source)
+            forward(k, source, 11 + i, along(k, 0, way(k)), action)
+
+    STAGES = (stage_last, stage_line, stage_next, stage_own)
+
+    def pass_tiles(k):
+        for i, stage in enumerate(STAGES):
+            ahead = k + DIRECT_A - 3 + i
+
+            @pl.when((ahead >= DIRECT_A) & (ahead < N))
+            def _():
+                stage(ahead, start, True)
+
+    def wait_tiles(k):
+        @pl.when(k < DIRECT_A)
+        def _():
+            def one(j, _):
+                @pl.when(j != me)
+                def _():
+                    tile_arrival(k, j).wait_recv()
+
+                return 0
+
+            lax.fori_loop(k, N, one, 0)
+
+        @pl.when(k >= DIRECT_A)
+        def _():
+            for i in range(4):
+                wait_tile(k, along(k, i, way(k)))
+                wait_tile(k, along(k, i, 2))
 
     def clear(k, _):
         high[at(k), :] = jnp.zeros((W, B + XW), BF16)
@@ -158,57 +251,50 @@
 
     lax.fori_loop(0, N, clear, 0)
 
-    own_bit = (y // 2, z // 2, z // 2)
-
-    def slot(d, k):
-        return d * N + k if d < FULL else FULL * N + (d - FULL) * (N // 2) + k // 2
-
-    def x_copy(d, k):
+    def x_copy(d, k, parity):
+        parent = TREES[parity][d][0] if parity is not None else -1
+        dz, dy = OFFSETS[d]
+        if parent >= 0:
+            dz, dy = dz - OFFSETS[parent][0], dy - OFFSETS[parent][1]
         return pltpu.make_async_remote_copy(
-            src_ref=x_own.at[at(k)], dst_ref=x_got.at[slot(d, k)],
-            send_sem=x_send.at[slot(d, k)], recv_sem=x_recv.at[slot(d, k)],
-            device_id={"tm": tm, "col": moved(*OFFSETS[d])}, device_id_type=MESH,
+            src_ref=x_own.at[at(k)] if parent < 0 else x_got.at[parent * N + k],
+            dst_ref=x_got.at[d * N + k],
+            send_sem=x_send.at[d * N + k], recv_sem=x_recv.at[d * N + k],
+            device_id={"tm": tm, "col": moved(dz, dy)}, device_id_type=MESH,
         )
 
-    def updated(k, begin, width):
-        def add(kk, total):
-            return total + dot3(
-                high[at(k), at(kk, 2 * W)], low[at(k), at(kk, 2 * W)],
-                high[at(kk, 2 * W), pl.ds(begin, width)], low[at(kk, 2 * W), pl.ds(begin, width)],
-            )
-
-        return lax.fori_loop(0, (k + 1) // 2, add, jnp.zeros((W, width), F32))
-
-    def step(k, _):
-        def wait_tile(j, _):
-            @pl.when(j != me)
+    def pass_x(k, level):
+        for parity in range(2):
+
+            @pl.when((k >= 0) & (k < DIRECT_X) & (k % 2 == parity))
             def _():
-                tile_arrival(k, j).wait_recv()
-
+                tree = TREES[parity]
+                for d, (_, hops) in tree.items():
+                    if hops == level - 1 and d in PASSED[parity]:
+                        x_copy(d, k, parity).wait_recv()
+                for d, (_, hops) in tree.items():
+                    if hops == level:
+                        x_copy(d, k, parity).start()
+
+    def step(k, half):
+        rows = half * W
+        part_rows = pl.ds(pl.multiple_of(rows, W), W)
+        pass_tiles(k)
+        wait_tiles(k)
+
+        def subtract(j, _):
+            panel[part_rows, at(j)] = tiles[tile(k, j)] - panel[part_rows, at(j)]
             return 0
 
-        lax.fori_loop(k, N, wait_tile, 0)
-
-        def update_four(c, _):
-            begin = pl.multiple_of(c * 4 * W, 4 * W)
-            total = updated(k, begin, 4 * W)
-            for i in range(4):
-                j = c * 4 + i
-
-                @pl.when(j >= k)
-                def _():
-                    panel[:, at(j)] = tiles[tile(k, jnp.maximum(j, k))] - total[:, i * W : (i + 1) * W]
-
-            return 0
-
-        lax.fori_loop(k // 4, N // 4, update_four, 0)
-        total = updated(k, X0, XW)
-        panel[:, X0 : X0 + W] = left[at(k), :] - total[:, :W]
-        panel[:, X0 + W : X0 + 2 * W] = right[at(k), :] - total[:, W : 2 * W]
-        rows = jnp.concatenate([effects[:, at(k)], jnp.zeros((W - NF, W), F32)], axis=0)
-        panel[:, X0 + 2 * W :] = rows.T - total[:, 2 * W :]
-
-        upper, inverse = corner([panel[8 * i : 8 * i + 8, at(k)] for i in range(W // 8)])
+        lax.fori_loop(k, N, subtract, 0)
+        panel[part_rows, X0 : X0 + W] = left[at(k), :] - panel[part_rows, X0 : X0 + W]
+        panel[part_rows, X0 + W : X0 + 2 * W] = right[at(k), :] - panel[part_rows, X0 + W : X0 + 2 * W]
+        turned_rows = jnp.concatenate([effects[:, at(k)], jnp.zeros((W - NF, W), F32)], axis=0).T
+        panel[part_rows, X0 + 2 * W :] = turned_rows - panel[part_rows, X0 + 2 * W :]
+
+        upper, inverse = corner(
+            [panel[pl.ds(pl.multiple_of(rows + 8 * i, 8), 8), at(k)] for i in range(W // 8)]
+        )
         for i in range(W // 8):
             corner_up[8 * i : 8 * i + 8, :] = upper[i]
             corner_inv[8 * i : 8 * i + 8, :] = inverse[i]
@@ -221,7 +307,7 @@
 
         def solve_four(c, _):
             begin = pl.multiple_of(c * 4 * W, 4 * W)
-            part = dot3(inv_high, inv_low, *split(panel[:, pl.ds(begin, 4 * W)]))
+            part = dot3(inv_high, inv_low, *split(panel[part_rows, pl.ds(begin, 4 * W)]))
             for i in range(4):
                 j = c * 4 + i
 
@@ -239,24 +325,72 @@
             return 0
 
         lax.fori_loop(k // 4, N // 4, solve_four, 0)
-        part = dot3(inv_high, inv_low, *split(panel[:, X0:]))
+        part = dot3(inv_high, inv_low, *split(panel[part_rows, X0:]))
         x_own[at(k), :] = part[:, : 2 * W]
         high[at(k), X0:], low[at(k), X0:] = split(part)
+
+        pass_x(k, 1)
+
+        @pl.when(k >= DIRECT_X)
+        def _():
+            for d in range(PEERS):
+                x_copy(d, k, None).start()
+
+        for level in range(2, 5):
+            pass_x(k - level + 1, level)
+
         for i in range(3):
-            rows = slice(i * W, (i + 1) * W)
-            xt_high[rows, at(k)], xt_low[rows, at(k)] = split(part[:, rows].T)
-        for d in range(len(OFFSETS)):
-            if d < FULL:
-                x_copy(d, k).start()
-            else:
-
-                @pl.when((k + own_bit[d - FULL]) % 2 == 0)
-                def _():
-                    x_copy(d, k).start()
-
-        return 0
-
-    lax.fori_loop(0, N, step, 0)
+            cols = slice(i * W, (i + 1) * W)
+            xt_high[cols, at(k)], xt_low[cols, at(k)] = split(part[:, cols].T)
+
+        @pl.when(half == 0)
+        def _():
+            last_high, last_low = high[at(k + 1), at(k)], low[at(k + 1), at(k)]
+
+            def update_four(c, _):
+                cols = pl.ds(pl.multiple_of(c * 4 * W, 4 * W), 4 * W)
+                panel[W:, cols] += dot3(last_high, last_low, high[at(k), cols], low[at(k), cols])
+                return 0
+
+            lax.fori_loop(k // 4, N // 4, update_four, 0)
+            panel[W:, X0:] += dot3(last_high, last_low, high[at(k), X0:], low[at(k), X0:])
+
+    def two_steps(p, _):
+        def total(begin, width):
+            def add(kk, sum_):
+                return sum_ + dot3(
+                    high[at(p, 2 * W), at(kk, 2 * W)], low[at(p, 2 * W), at(kk, 2 * W)],
+                    high[at(kk, 2 * W), pl.ds(begin, width)], low[at(kk, 2 * W), pl.ds(begin, width)],
+                )
+
+            panel[:, pl.ds(begin, width)] = lax.fori_loop(0, p, add, jnp.zeros((2 * W, width), F32))
+
+        def update_two(c, _):
+            total(pl.multiple_of(c * 2 * W, 2 * W), 2 * W)
+            return 0
+
+        lax.fori_loop(p, N // 2, update_two, 0)
+        total(X0, XW)
+
+        def one_step(half, _):
+            step(2 * p + half, half)
+            return 0
+
+        lax.fori_loop(0, 2, one_step, 0)
+        return 0
+
+    lax.fori_loop(0, N // 2, two_steps, 0)
+    pass_x(DIRECT_X - 1, 4)
+
+    for k in range(DIRECT_A):
+        direct_tiles(k, wait_send)
+
+    def drain_tiles(k, _):
+        for stage in STAGES:
+            stage(k, wait_send, False)
+        return 0
+
+    lax.fori_loop(DIRECT_A, N, drain_tiles, 0)
 
     self_gram[...] = jnp.zeros((XW, XW), F32)
 
@@ -264,28 +398,26 @@
         tiles[i] = jnp.zeros((W, W), F32)
         return 0
 
-    lax.fori_loop(0, 4 * len(OFFSETS), clear_gram, 0)
-
-    def add_gram(d, k, got):
-        part = dot3(xt_high[: 2 * W, k], xt_low[: 2 * W, k], *split(got))
-        tiles[4 * d] += part[:W, :W]
-        tiles[4 * d + 1] += part[:W, W:]
-        tiles[4 * d + 2] += part[W:, W:]
-        tiles[4 * d + 3] += part[W:, :W]
+    lax.fori_loop(0, 4 * PEERS, clear_gram, 0)
 
     def gram_step(p, _):
         pair = at(p, 2 * W)
         self_gram[...] += dot3(xt_high[:, pair], xt_low[:, pair], high[pair, X0:], low[pair, X0:])
-        for d in range(len(OFFSETS)):
-            if d < FULL:
-                x_copy(d, 2 * p).wait_recv()
-                x_copy(d, 2 * p + 1).wait_recv()
-                got = x_got[pl.ds(d * N + 2 * p, 2)].reshape(2 * W, 2 * W)
-                add_gram(d, pair, got)
-            else:
-                k = 2 * p + 1 - own_bit[d - FULL]
-                x_copy(d, k).wait_recv()
-                add_gram(d, at(k), x_got[slot(d, k)])
+        for d in range(PEERS):
+            for half in range(2):
+                if d in PASSED[half]:
+
+                    @pl.when(2 * p >= DIRECT_X)
+                    def _():
+                        x_copy(d, 2 * p + half, None).wait_recv()
+                else:
+                    x_copy(d, 2 * p + half, None).wait_recv()
+            got = x_got[pl.ds(d * N + 2 * p, 2)].reshape(2 * W, 2 * W)
+            part = dot3(xt_high[: 2 * W, pair], xt_low[: 2 * W, pair], *split(got))
+            tiles[4 * d] += part[:W, :W]
+            tiles[4 * d + 1] += part[:W, W:]
+            tiles[4 * d + 2] += part[W:, W:]
+            tiles[4 * d + 3] += part[W:, :W]
         return 0
 
     lax.fori_loop(0, N // 2, gram_step, 0)
@@ -298,7 +430,7 @@
             device_id={"tm": tm, "col": moved(-dz, -dy)}, device_id_type=MESH,
         )
 
-    for d in range(len(OFFSETS)):
+    for d in range(BACK):
         result_copy(d).start()
 
     cross_own[...] = self_gram[2 * W : 2 * W + NF, :W]
@@ -324,7 +456,8 @@
     def _():
         cross_copy.start()
 
-    base = 4 * len(OFFSETS)
+    separator_copy.wait()
+    base = 4 * PEERS
 
     def next_copy(b):
         return pltpu.make_async_remote_copy(
@@ -341,18 +474,15 @@
             next_copy(b).start()
 
         coupling_out[at(b), :] = -cross_gram
-        diagonal_out[at(b), :] = separator[at(b), :] - right_gram
+        diagonal_out[at(b), :] -= right_gram
 
     block_out(me, self_gram[:W, :W], self_gram[:W, W : 2 * W], self_gram[W : 2 * W, W : 2 * W])
-    for d in range(FULL):
+    for d in range(PEERS):
         dz, dy = OFFSETS[d]
         block_out(moved(-dz, -dy), tiles[4 * d].T, tiles[4 * d + 3].T, tiles[4 * d + 2].T)
-    for d in range(len(OFFSETS)):
+    for d in range(BACK):
         result_copy(d).wait_recv()
-        got = [result_got[d, i] for i in range(3)]
-        if d >= FULL:
-            got = [got[0] + tiles[4 * d].T, got[1] + tiles[4 * d + 3].T, got[2] + tiles[4 * d + 2].T]
-        block_out(moved(*OFFSETS[d]), *got)
+        block_out(moved(*OFFSETS[d]), result_got[d, 0], result_got[d, 1], result_got[d, 2])
 
     total = self_gram[2 * W : 2 * W + NF, 2 * W :]
     for o in range(1, tms):
@@ -374,30 +504,14 @@
 
         lax.fori_loop(0, N, add_next, 0)
 
-    def drain_tiles(k, _):
-        def one(o, _):
-            tile_copy(k, o).wait_send()
+    for d in range(PEERS):
+
+        def drain_x(k, _):
+            x_copy(d, k, None).wait_send()
             return 0
 
-        lax.fori_loop(1, N, one, 0)
-        return 0
-
-    lax.fori_loop(0, me + 1, drain_tiles, 0)
-    for d in range(len(OFFSETS)):
-        if d < FULL:
-
-            def drain_x(k, _):
-                x_copy(d, k).wait_send()
-                return 0
-
-            lax.fori_loop(0, N, drain_x, 0)
-        else:
-
-            def drain_half(p, _):
-                x_copy(d, 2 * p + own_bit[d - FULL]).wait_send()
-                return 0
-
-            lax.fori_loop(0, N // 2, drain_half, 0)
+        lax.fori_loop(0, N, drain_x, 0)
+    for d in range(BACK):
         result_copy(d).wait_send()
     for o in range(1, tms):
         tip_copy(o).wait_send()
@@ -416,7 +530,7 @@
 def local(interior, left, right, effects, separator, separator_effects, tip):
     tms = lax.axis_size("tm")
     dma = pltpu.SemaphoreType.DMA
-    copies = FULL * N + 3 * (N // 2)
+    copies = PEERS * N
     vmem = pl.BlockSpec(memory_space=pltpu.VMEM)
     outputs = pl.pallas_call(
         kernel,
@@ -427,13 +541,13 @@
             jax.ShapeDtypeStruct((NF, W), F32),
             jax.ShapeDtypeStruct((NF, NF), F32),
         ),
-        in_specs=[vmem] * 7,
+        in_specs=[vmem] * 4 + [pl.BlockSpec(memory_space=pl.ANY)] + [vmem] * 2,
         out_specs=[vmem] * 5,
         scratch_shapes=[
             pltpu.VMEM((TILES, W, W), F32),
             pltpu.VMEM((B, B + XW), BF16),
             pltpu.VMEM((B, B + XW), BF16),
-            pltpu.VMEM((W, B + XW), F32),
+            pltpu.VMEM((2 * W, B + XW), F32),
             pltpu.VMEM((W, W), F32),
             pltpu.VMEM((W, W), F32),
             pltpu.VMEM((B, 2 * W), F32),
@@ -441,7 +555,7 @@
             pltpu.VMEM((XW, B), BF16),
             pltpu.VMEM((XW, B), BF16),
             pltpu.VMEM((XW, XW), F32),
-            pltpu.VMEM((len(OFFSETS), 3, W, W), F32),
+            pltpu.VMEM((BACK, 3, W, W), F32),
             pltpu.VMEM((N, W, W), F32),
             pltpu.VMEM((NF, W), F32),
             pltpu.VMEM((8, NF, W), F32),
@@ -451,14 +565,15 @@
             dma((TILES,)),
             dma((copies,)),
             dma((copies,)),
-            dma((len(OFFSETS),)),
-            dma((len(OFFSETS),)),
+            dma((BACK,)),
+            dma((BACK,)),
             dma((N,)),
             dma((N,)),
             dma(()),
             dma(()),
             dma((8,)),
             dma((8,)),
+            dma(()),
         ],
         compiler_params=pltpu.CompilerParams(
             collective_id=0, has_side_effects=True, vmem_limit_bytes=64 * 1024 * 1024 - 65536

time: 450 us -> 348 us (0.77); the launches traced: 444 us -> 348 us
  Pallas kernels: 437 us -> 341 us
    pallas_call x1, Pallas kernels: 437 us -> 341 us  [local(): pl.pallas_call(kernel, out_shape=(jax.ShapeDtypeStruct((B, W), F32), jax....]
where the time goes in v2:
time: 348 us
  Pallas kernels  341 us (98%)
  local copies, waits for them, and re-layouts  6.31 us (2%)
    pallas_call x1, Pallas kernels, local(): pl.pallas_call(kernel, out_shape=(jax.ShapeDtypeStruct((B, W), F32), jax....  341 us

profile of v2, /device:TPU:97, one launch (start us, length us, event | category | flops | bytes accessed | tf_op | source)
XLA Modules:
  0.0 347.7 jit_solution(2924702403527771768)
XLA Ops:
  0.6 340.7 %eliminate.1 = (f32[2048,128]{1,0:T(8,128)}, f32[2048,128]{1,0:T(8,128)}, f32[2048,128]{1,0:T(8,128)}, f32[64,128]{1,0:T(8,128)}, f32[64,64]{1,0:T(8,128)}) custom-call(f32[2048,128]{1,0:T(8,128)} %bitcast.13, f32[2048,128]{1,0:T(8,128)} %bitcast.14, f32[2048,128]{1,0:T(8,128)} %bitcast.15, f32[64,2048]{1,0:T(8,128)} %bitcast.17, f32[2048,128]{1,0:T(8,128)} %bitcast.16, ...), custom_call_target="tpu_custom_call" | custom-call | tf_op jit(solution)/shard_map/eliminate/pallas_call | solution.py:535
  341.4 0.0 copy-start.1
  341.4 2.4 copy.17
  343.7 0.0 copy-done.1
  343.7 0.0 copy-start
  343.7 1.0 copy.18
  344.7 0.6 copy-done
  345.3 0.0 copy-start.3
  345.3 1.0 copy.19
  346.3 0.0 copy-done.3
  346.3 0.0 copy-start.2
  346.3 0.6 copy.20
  346.9 0.2 copy-done.2
  347.1 0.6 copy.21
Async XLA Ops:
  341.4 2.4 copy-start.1
  343.7 1.6 copy-start
  345.3 1.0 copy-start.3
  346.3 0.8 copy-start.2

commit v3 on v2

--- a/solution.py
+++ b/solution.py
@@ -23,7 +23,7 @@
 )
 PASSED = tuple(frozenset(p for p, _ in tree.values()) for tree in TREES)
 DIRECT_X = 14
-DIRECT_A = 5
+DIRECT_A = 1
 
 
 def split(x):
@@ -167,9 +167,6 @@
     def wait_send(copy):
         copy.wait_send()
 
-    for k in range(DIRECT_A):
-        direct_tiles(k, start)
-
     def along(k, first, second):
         even = 1 - k % 2
         dz = first * (1 - even) + second * even
@@ -217,13 +214,17 @@
 
     STAGES = (stage_last, stage_line, stage_next, stage_own)
 
+    for k in range(DIRECT_A, DIRECT_A + 3):
+        stage_own(k, start, True)
+    for k in range(DIRECT_A):
+        direct_tiles(k, start)
+
     def pass_tiles(k):
         for i, stage in enumerate(STAGES):
-            ahead = k + DIRECT_A - 3 + i
-
-            @pl.when((ahead >= DIRECT_A) & (ahead < N))
+
+            @pl.when(k + 1 + i < N)
             def _():
-                stage(ahead, start, True)
+                stage(k + 1 + i, start, True)
 
     def wait_tiles(k):
         @pl.when(k < DIRECT_A)
@@ -250,6 +251,10 @@
         return 0
 
     lax.fori_loop(0, N, clear, 0)
+
+    stage_next(DIRECT_A, start, True)
+    stage_next(DIRECT_A + 1, start, True)
+    stage_line(DIRECT_A, start, True)
 
     def x_copy(d, k, parity):
         parent = TREES[parity][d][0] if parity is not None else -1
@@ -305,6 +310,20 @@
 
         inv_high, inv_low = split(corner_inv[...])
 
+        part = dot3(inv_high, inv_low, *split(panel[part_rows, X0:]))
+        x_own[at(k), :] = part[:, : 2 * W]
+        high[at(k), X0:], low[at(k), X0:] = split(part)
+
+        pass_x(k, 1)
+
+        @pl.when(k >= DIRECT_X)
+        def _():
+            for d in range(PEERS):
+                x_copy(d, k, None).start()
+
+        for level in range(2, 5):
+            pass_x(k - level + 1, level)
+
         def solve_four(c, _):
             begin = pl.multiple_of(c * 4 * W, 4 * W)
             part = dot3(inv_high, inv_low, *split(panel[part_rows, pl.ds(begin, 4 * W)]))
@@ -324,21 +343,7 @@
 
             return 0
 
-        lax.fori_loop(k // 4, N // 4, solve_four, 0)
-        part = dot3(inv_high, inv_low, *split(panel[part_rows, X0:]))
-        x_own[at(k), :] = part[:, : 2 * W]
-        high[at(k), X0:], low[at(k), X0:] = split(part)
-
-        pass_x(k, 1)
-
-        @pl.when(k >= DIRECT_X)
-        def _():
-            for d in range(PEERS):
-                x_copy(d, k, None).start()
-
-        for level in range(2, 5):
-            pass_x(k - level + 1, level)
-
+        lax.fori_loop((k + 1) // 4, N // 4, solve_four, 0)
         for i in range(3):
             cols = slice(i * W, (i + 1) * W)
             xt_high[cols, at(k)], xt_low[cols, at(k)] = split(part[:, cols].T)

time: 348 us -> 322 us (0.925); the launches traced: 348 us -> 316 us
  Pallas kernels: 341 us -> 309 us
    pallas_call x1, Pallas kernels: 341 us -> 309 us  [local(): pl.pallas_call(kernel, out_shape=(jax.ShapeDtypeStruct((B, W), F32), jax....]
where the time goes in v3:
time: 322 us; the launch traced here: 316 us
  Pallas kernels  309 us (96%)
  local copies, waits for them, and re-layouts  6.31 us (2%)
    pallas_call x1, Pallas kernels, local(): pl.pallas_call(kernel, out_shape=(jax.ShapeDtypeStruct((B, W), F32), jax....  309 us

profile of v3, /device:TPU:97, one launch (start us, length us, event | category | flops | bytes accessed | tf_op | source)
XLA Modules:
  0.0 315.7 jit_solution(3734640607337927732)
XLA Ops:
  0.6 308.8 %eliminate.1 = (f32[2048,128]{1,0:T(8,128)}, f32[2048,128]{1,0:T(8,128)}, f32[2048,128]{1,0:T(8,128)}, f32[64,128]{1,0:T(8,128)}, f32[64,64]{1,0:T(8,128)}) custom-call(f32[2048,128]{1,0:T(8,128)} %bitcast.13, f32[2048,128]{1,0:T(8,128)} %bitcast.14, f32[2048,128]{1,0:T(8,128)} %bitcast.15, f32[64,2048]{1,0:T(8,128)} %bitcast.17, f32[2048,128]{1,0:T(8,128)} %bitcast.16, ...), custom_call_target="tpu_custom_call" | custom-call | tf_op jit(solution)/shard_map/eliminate/pallas_call | solution.py:540
  309.4 0.0 copy-start.1
  309.4 2.4 copy.17
  311.8 0.0 copy-done.1
  311.8 0.0 copy-start
  311.8 1.0 copy.18
  312.7 0.6 copy-done
  313.4 0.0 copy-start.3
  313.4 1.0 copy.19
  314.3 0.0 copy-done.3
  314.3 0.0 copy-start.2
  314.3 0.6 copy.20
  315.0 0.2 copy-done.2
  315.1 0.6 copy.21
Async XLA Ops:
  309.4 2.4 copy-start.1
  311.8 1.6 copy-start
  313.4 1.0 copy-start.3
  314.3 0.8 copy-start.2

commit v4 on v3

--- a/solution.py
+++ b/solution.py
@@ -22,7 +22,6 @@
     {1: (-1, 1), 2: (1, 2), 3: (1, 2), 0: (2, 3), 4: (3, 3), 5: (2, 3), 6: (4, 4), 7: (5, 4), 8: (4, 4)},
 )
 PASSED = tuple(frozenset(p for p, _ in tree.values()) for tree in TREES)
-DIRECT_X = 14
 DIRECT_A = 1
 
 
@@ -32,10 +31,9 @@
 
 
 def dot3(a_high, a_low, b_high, b_low):
-    def one(a, b):
-        return jnp.dot(a, b, preferred_element_type=F32)
-
-    return one(a_high, b_high) + (one(a_high, b_low) + one(a_low, b_high))
+    left = jnp.concatenate([a_high, a_high, a_low], axis=1)
+    right = jnp.concatenate([b_high, b_low, b_high], axis=0)
+    return jnp.dot(left, right, preferred_element_type=F32)
 
 
 def corner(rows):
@@ -271,7 +269,7 @@
     def pass_x(k, level):
         for parity in range(2):
 
-            @pl.when((k >= 0) & (k < DIRECT_X) & (k % 2 == parity))
+            @pl.when((k >= 0) & (k < N) & (k % 2 == parity))
             def _():
                 tree = TREES[parity]
                 for d, (_, hops) in tree.items():
@@ -316,11 +314,6 @@
 
         pass_x(k, 1)
 
-        @pl.when(k >= DIRECT_X)
-        def _():
-            for d in range(PEERS):
-                x_copy(d, k, None).start()
-
         for level in range(2, 5):
             pass_x(k - level + 1, level)
 
@@ -385,7 +378,6 @@
         return 0
 
     lax.fori_loop(0, N // 2, two_steps, 0)
-    pass_x(DIRECT_X - 1, 4)
 
     for k in range(DIRECT_A):
         direct_tiles(k, wait_send)
@@ -410,12 +402,7 @@
         self_gram[...] += dot3(xt_high[:, pair], xt_low[:, pair], high[pair, X0:], low[pair, X0:])
         for d in range(PEERS):
             for half in range(2):
-                if d in PASSED[half]:
-
-                    @pl.when(2 * p >= DIRECT_X)
-                    def _():
-                        x_copy(d, 2 * p + half, None).wait_recv()
-                else:
+                if d not in PASSED[half]:
                     x_copy(d, 2 * p + half, None).wait_recv()
             got = x_got[pl.ds(d * N + 2 * p, 2)].reshape(2 * W, 2 * W)
             part = dot3(xt_high[: 2 * W, pair], xt_low[: 2 * W, pair], *split(got))
@@ -425,7 +412,15 @@
             tiles[4 * d + 3] += part[W:, :W]
         return 0
 
-    lax.fori_loop(0, N // 2, gram_step, 0)
+    lax.fori_loop(0, 2, gram_step, 0)
+    for level in range(2, 5):
+        pass_x(N - level + 1, level)
+    lax.fori_loop(2, 4, gram_step, 0)
+    for level in range(3, 5):
+        pass_x(N - level + 2, level)
+    lax.fori_loop(4, 6, gram_step, 0)
+    pass_x(N - 1, 4)
+    lax.fori_loop(6, N // 2, gram_step, 0)
 
     def result_copy(d):
         dz, dy = OFFSETS[d]

time: 322 us -> 283 us (0.88)
  Pallas kernels: 309 us -> 271 us
    pallas_call x1, Pallas kernels: 309 us -> 271 us  [local(): pl.pallas_call(kernel, out_shape=(jax.ShapeDtypeStruct((B, W), F32), jax....]
where the time goes in v4:
time: 283 us; the launch traced here: 278 us
  Pallas kernels  271 us (96%)
  local copies, waits for them, and re-layouts  6.31 us (2%)
    pallas_call x1, Pallas kernels, local(): pl.pallas_call(kernel, out_shape=(jax.ShapeDtypeStruct((B, W), F32), jax....  271 us
    unnamed x13, local copies, waits for them, and re-layouts  6.31 us

profile of v4, /device:TPU:97, one launch (start us, length us, event | category | flops | bytes accessed | tf_op | source)
XLA Modules:
  0.0 278.3 jit_solution(8021553789622734545)
XLA Ops:
  0.6 271.4 %eliminate.1 = (f32[2048,128]{1,0:T(8,128)}, f32[2048,128]{1,0:T(8,128)}, f32[2048,128]{1,0:T(8,128)}, f32[64,128]{1,0:T(8,128)}, f32[64,64]{1,0:T(8,128)}) custom-call(f32[2048,128]{1,0:T(8,128)} %bitcast.13, f32[2048,128]{1,0:T(8,128)} %bitcast.14, f32[2048,128]{1,0:T(8,128)} %bitcast.15, f32[64,2048]{1,0:T(8,128)} %bitcast.17, f32[2048,128]{1,0:T(8,128)} %bitcast.16, ...), custom_call_target="tpu_custom_call" | custom-call | tf_op jit(solution)/shard_map/eliminate/pallas_call | solution.py:535
  272.0 0.0 copy-start.1
  272.0 2.4 copy.17
  274.4 0.0 copy-done.1
  274.4 0.0 copy-start
  274.4 1.0 copy.18
  275.3 0.6 copy-done
  276.0 0.0 copy-start.3
  276.0 1.0 copy.19
  277.0 0.0 copy-done.3
  277.0 0.0 copy-start.2
  277.0 0.6 copy.20
  277.6 0.2 copy-done.2
  277.7 0.6 copy.21
Async XLA Ops:
  272.0 2.4 copy-start.1
  274.4 1.6 copy-start
  276.0 1.0 copy-start.3
  277.0 0.8 copy-start.2

commit v5 on v4

--- a/solution.py
+++ b/solution.py
@@ -22,7 +22,6 @@
     {1: (-1, 1), 2: (1, 2), 3: (1, 2), 0: (2, 3), 4: (3, 3), 5: (2, 3), 6: (4, 4), 7: (5, 4), 8: (4, 4)},
 )
 PASSED = tuple(frozenset(p for p, _ in tree.values()) for tree in TREES)
-DIRECT_A = 1
 
 
 def split(x):
@@ -149,16 +148,6 @@
 
     lax.fori_loop(0, me + 1, own_tile, 0)
 
-    def direct_tiles(k, action):
-        @pl.when(me >= k)
-        def _():
-            def to_one(o, _):
-                to = ((z + o // 4) % 4) * 4 + (y + o % 4) % 4
-                action(tile_copy(k, me, o - 1, to))
-                return 0
-
-            lax.fori_loop(1, N, to_one, 0)
-
     def start(copy):
         copy.start()
 
@@ -212,10 +201,8 @@
 
     STAGES = (stage_last, stage_line, stage_next, stage_own)
 
-    for k in range(DIRECT_A, DIRECT_A + 3):
+    for k in range(4):
         stage_own(k, start, True)
-    for k in range(DIRECT_A):
-        direct_tiles(k, start)
 
     def pass_tiles(k):
         for i, stage in enumerate(STAGES):
@@ -225,22 +212,9 @@
                 stage(k + 1 + i, start, True)
 
     def wait_tiles(k):
-        @pl.when(k < DIRECT_A)
-        def _():
-            def one(j, _):
-                @pl.when(j != me)
-                def _():
-                    tile_arrival(k, j).wait_recv()
-
-                return 0
-
-            lax.fori_loop(k, N, one, 0)
-
-        @pl.when(k >= DIRECT_A)
-        def _():
-            for i in range(4):
-                wait_tile(k, along(k, i, way(k)))
-                wait_tile(k, along(k, i, 2))
+        for i in range(4):
+            wait_tile(k, along(k, i, way(k)))
+            wait_tile(k, along(k, i, 2))
 
     def clear(k, _):
         high[at(k), :] = jnp.zeros((W, B + XW), BF16)
@@ -250,9 +224,9 @@
 
     lax.fori_loop(0, N, clear, 0)
 
-    stage_next(DIRECT_A, start, True)
-    stage_next(DIRECT_A + 1, start, True)
-    stage_line(DIRECT_A, start, True)
+    for stage, panels in ((stage_next, 3), (stage_line, 2), (stage_last, 1)):
+        for k in range(panels):
+            stage(k, start, True)
 
     def x_copy(d, k, parity):
         parent = TREES[parity][d][0] if parity is not None else -1
@@ -379,15 +353,12 @@
 
     lax.fori_loop(0, N // 2, two_steps, 0)
 
-    for k in range(DIRECT_A):
-        direct_tiles(k, wait_send)
-
     def drain_tiles(k, _):
         for stage in STAGES:
             stage(k, wait_send, False)
         return 0
 
-    lax.fori_loop(DIRECT_A, N, drain_tiles, 0)
+    lax.fori_loop(0, N, drain_tiles, 0)
 
     self_gram[...] = jnp.zeros((XW, XW), F32)
 

time: 283 us -> 270 us (0.954); the launches traced: 278 us -> 269 us
  Pallas kernels: 271 us -> 262 us
    pallas_call x1, Pallas kernels: 271 us -> 262 us  [local(): pl.pallas_call(kernel, out_shape=(jax.ShapeDtypeStruct((B, W), F32), jax....]
where the time goes in v5:
time: 270 us; the launch traced here: 269 us
  Pallas kernels  262 us (97%)
  local copies, waits for them, and re-layouts  6.31 us (2%)
    pallas_call x1, Pallas kernels, local(): pl.pallas_call(kernel, out_shape=(jax.ShapeDtypeStruct((B, W), F32), jax....  262 us
    unnamed x13, local copies, waits for them, and re-layouts  6.31 us

profile of v5, /device:TPU:97, one launch (start us, length us, event | category | flops | bytes accessed | tf_op | source)
XLA Modules:
  0.0 269.0 jit_solution(10377825791919652597)
XLA Ops:
  0.6 262.1 %eliminate.1 = (f32[2048,128]{1,0:T(8,128)}, f32[2048,128]{1,0:T(8,128)}, f32[2048,128]{1,0:T(8,128)}, f32[64,128]{1,0:T(8,128)}, f32[64,64]{1,0:T(8,128)}) custom-call(f32[2048,128]{1,0:T(8,128)} %bitcast.13, f32[2048,128]{1,0:T(8,128)} %bitcast.14, f32[2048,128]{1,0:T(8,128)} %bitcast.15, f32[64,2048]{1,0:T(8,128)} %bitcast.17, f32[2048,128]{1,0:T(8,128)} %bitcast.16, ...), custom_call_target="tpu_custom_call" | custom-call | tf_op jit(solution)/shard_map/eliminate/pallas_call | solution.py:506
  262.7 0.0 copy-start.1
  262.7 2.4 copy.17
  265.1 0.0 copy-done.1
  265.1 0.0 copy-start
  265.1 1.0 copy.18
  266.0 0.6 copy-done
  266.7 0.0 copy-start.3
  266.7 1.0 copy.19
  267.6 0.0 copy-done.3
  267.6 0.0 copy-start.2
  267.6 0.6 copy.20
  268.3 0.2 copy-done.2
  268.4 0.6 copy.21
Async XLA Ops:
  262.7 2.4 copy-start.1
  265.1 1.6 copy-start
  266.7 1.0 copy-start.3
  267.6 0.8 copy-start.2
